TPU v7x, 32 devices: a whole 2x2x4 slice. The times are simulated.
32 devices in a mesh: groups: 2 (over y), date: 4 (over z), tile: 2 (over x), head: 2 (over core).
Axes of the slice: x: 2, y: 2, z: 4, core: 2. Of those that a mesh axis runs over, the one named last changes fastest.
Arguments:
- tokens: bfloat16 [8, 8, 8, 64, 256], P('groups', 'tile', None, 'date'), parts along dimension 0, may hold values from -240 to 240
- cloud_mask: int32 [8, 8, 8, 64], P('groups', 'tile', None, 'date'), parts along dimension 0, may hold values from 0 to 1, as said below
- day_of_year: int32 [128], P(('groups', 'date')), parts along dimension 0, may hold values from 0 to 1460
- query: float32 [256], P('head'), may hold values from -6 to 6
- key_weight: bfloat16 [256, 256], P(None, 'head'), may hold values from -0.375 to 0.375
- value_weight: bfloat16 [256, 256], P(None, 'head'), may hold values from -0.375 to 0.375
- conv_first: bfloat16 [3, 3, 256, 256], P(None, None, None, 'head'), may hold values from -0.375 to 0.375
- conv_second: bfloat16 [3, 3, 256, 256], P(None, None, None, 'head'), may hold values from -0.1875 to 0.1875
Outputs:
- feature_map: bfloat16 [8, 8, 8, 256], P(('groups', 'date'), 'tile', None, 'head'), parts along dimension 0
There are 2 independent parts, one for each index of `groups`. A program takes and returns all parts, laid end to end along the dimension named above; an argument that names none is the same for every part. Nothing has to cross between parts.
Inputs may be any that keep to these rules, and one draw needn't show every extreme that they name: `cloud_mask`: a pixel may be clouded on all 64 dates.
All inputs are finite; a program needn't handle non-finite values.
Results may differ from a plain program's by a relative error of at most 0.012.
The roundings to bfloat16 on the way count: a program that leaves them out, or rounds other values in their place, can miss the bound.
Values may be sent and summed in bfloat16 or wider, within the bound.
A program may use at most 128 MiB of HBM per device.

v0:
```python
import jax
import jax.numpy as jnp
from jax import lax
from jax.sharding import PartitionSpec as P

HSIZE = 32
TILE_DEV = 1


cloud_penalty = 6.0


def with_halo(block, sides, width):
    for axis, dim in sides:
        count = lax.axis_size(axis)
        forward = [(i, i + 1) for i in range(count - 1)]
        backward = [(target, source) for source, target in forward]
        low = lax.ppermute(
            lax.slice_in_dim(block, block.shape[dim] - width, None, axis=dim), axis, forward
        )
        high = lax.ppermute(lax.slice_in_dim(block, 0, width, axis=dim), axis, backward)
        block = jnp.concatenate([low, block, high], axis=dim)
    return block


def encoding(day_of_year, width):
    chan = jnp.arange(width)
    expo = (2 * (chan // 2)).astype(jnp.float32) / width
    freq = jnp.power(jnp.float32(1000.0), -expo)
    angle = day_of_year.astype(jnp.float32)[:, None] * freq[None, :]
    return jnp.where((chan % 2 == 0)[None, :], jnp.sin(angle), jnp.cos(angle))


def widen(scales):
    return jnp.repeat(scales, HSIZE, axis=-1)


def merge_blocks(tops, tots, parts):
    best = jnp.max(tops, axis=0)
    scales = jnp.exp(tops - best[None])
    own_totals = jnp.sum(tots * scales, axis=0)
    own_sums = jnp.sum(parts * widen(scales), axis=0)
    return (own_totals, own_sums)


def convolve(block, kernel):
    rows, cols = (block.shape[1], block.shape[2])
    padded = with_halo(block, (("tile", 1),), 1)
    whole = lax.all_gather(padded, "head", axis=3, tiled=True)
    whole = jnp.pad(whole, ((0, 0), (0, 0), (1, 1), (0, 0)))
    total = jnp.zeros((block.shape[0] * rows * cols, kernel.shape[3]), jnp.float32)
    for arow in range(3):
        for bcol in range(3):
            piece = whole[:, arow : arow + rows, bcol : bcol + cols, :].reshape(-1, whole.shape[3])
            total = total + jnp.dot(piece, kernel[arow, bcol], preferred_element_type=jnp.float32)
    return total.reshape(block.shape[0], rows, cols, kernel.shape[3])


def local(
    tokens, cloud_mask, day_of_year, query, key_weight, value_weight, conv_first, conv_second
):
    tiles, rows, cols, dates, width = tokens.shape
    heads_dev = query.shape[0] // HSIZE
    table = encoding(day_of_year, width)
    inputs = (
        (tokens.astype(jnp.float32) + table[None, None, None])
        .astype(jnp.bfloat16)
        .reshape(-1, width)
    )
    keys = jnp.dot(inputs, key_weight, preferred_element_type=jnp.float32).reshape(
        tiles, rows, cols, dates, heads_dev, HSIZE
    )
    vals = jnp.dot(inputs, value_weight, preferred_element_type=jnp.float32).reshape(
        tiles, rows, cols, dates, heads_dev, HSIZE
    )
    query_heads = query.reshape(heads_dev, HSIZE)
    score = jnp.sum(keys * query_heads, axis=-1) / jnp.sqrt(jnp.float32(HSIZE))
    score = score - cloud_penalty * (1.0 - cloud_mask[..., None].astype(jnp.float32))
    top = jnp.max(score, axis=3)
    expo = jnp.exp(score - top[:, :, :, None, :])
    totals = jnp.sum(expo, axis=3)
    sums = jnp.sum(expo[..., None] * vals, axis=3).reshape(tiles, rows, cols, heads_dev * HSIZE)
    got = (
        lax.all_to_all(top, "date", split_axis=0, concat_axis=0, tiled=True),
        lax.all_to_all(totals, "date", split_axis=0, concat_axis=0, tiled=True),
        lax.all_to_all(sums, "date", split_axis=0, concat_axis=0, tiled=True),
    )
    sources = got[0].shape[0] // TILE_DEV
    tops = got[0].reshape(sources, TILE_DEV, rows, cols, heads_dev)
    tots = got[1].reshape(sources, TILE_DEV, rows, cols, heads_dev)
    parts = got[2].reshape(sources, TILE_DEV, rows, cols, heads_dev * HSIZE)
    own_totals, own_sums = merge_blocks(tops, tots, parts)
    pooled = (own_sums / widen(own_totals)).astype(jnp.bfloat16)
    hidden = jax.nn.relu(convolve(pooled, conv_first)).astype(jnp.bfloat16)
    return convolve(hidden, conv_second).astype(jnp.bfloat16)


def solution(mesh):
    in_specs = (
        P("groups", "tile", None, "date", None),
        P("groups", "tile", None, "date"),
        P(("groups", "date")),
        P("head"),
        P(None, "head"),
        P(None, "head"),
        P(None, None, None, "head"),
        P(None, None, None, "head"),
    )
    out_specs = P(("groups", "date"), "tile", None, "head")
    return jax.shard_map(local, mesh=mesh, in_specs=in_specs, out_specs=out_specs, check_vma=False)
```

profile of v0, /device:TPU:0, one launch (start us, length us, event | category | flops | bytes accessed | tf_op | source)
XLA Modules:
  0.0 57.5 jit_solution(14288607514884827071)
XLA Ops:
  0.0 0.9 %copy.23 = bf16[256,128]{0,1:T(8,128)(2,1)S(1)} copy(bf16[256,128]{1,0:T(8,128)(2,1)} %param.12) | data formatting | bytes 131072 | tf_op args[4]
  1.0 0.7 %mul.62 = f32[4,32]{1,0:T(4,128)S(1)} reshape(f32[128]{0:T(128)} %param.11) | data formatting | bytes 1024 | tf_op jit(solution)/shard_map/mul | solution.py:77
  1.7 0.7 %convert_element_type.63 = f32[16]{0:T(128)S(1)} convert(s32[16]{0:T(128)} %param.10) | non-fusion elementwise | flops 16 | bytes 128 | tf_op jit(solution)/shard_map/convert_element_type | solution.py:30
  2.4 0.8 %subtract_multiply_fusion = f32[4,4,8,16]{3,2,1,0:T(8,128)S(1)} fusion(s32[4,4,8,16]{3,2,1,0:T(8,128)} %param.9), kind=kLoop, calls=%fused_computation.79 | loop fusion | flops 6144 | bytes 16384 | tf_op jit(solution)/shard_map/mul | solution.py:78
  3.2 0.1 fusion.47
  3.4 2.6 %multiply_reduce_fusion.1 = f32[4,4,8,16,4]{3,4,2,1,0:T(4,128)S(1)} fusion(bf16[4,32,256,1,1,1]{2,1,0,5,4,3:T(8,128)(2,1)S(1)} %bitcast.147, f32[4,32]{1,0:T(4,128)S(1)} %mul.62, bf16[4,4,8,16,256]{4,3,2,1,0:T(8,128)(2,1)} %param.8, f32[16,256]{1,0:T(8,128)S(1)} %fusion.47), kind=kOutput, calls=%fused_computation.1 | convolution fusion | flops 136306688 | bytes 1163776 | tf_op jit(solution)/shard_map/dot_general | solution.py:70
  6.0 0.0 copy-start.2
  6.0 0.0 copy-start.3
  6.0 0.2 fusion.8
  6.3 0.2 copy.25
  6.4 0.7 %reshape.252 = f32[4,1,128]{2,1,0:T(1,128)} reshape(f32[4,4,4,8]{3,2,1,0:T(4,128)S(1)} %bitcast.146) | data formatting | bytes 4096
  7.1 6.3 %all-to-all-start.1 = ((f32[4,1,128]{2,1,0:T(1,128)}), f32[4,1,128]{2,1,0:T(1,128)S(1)}, u32[]{:S(2)}, u32[]{:S(2)}) async-start(f32[4,1,128]{2,1,0:T(1,128)} %reshape.252), calls=%async_computation.1 | async-start | bytes 4096 | tf_op jit(solution)/shard_map/all_to_all | solution.py:84
  13.4 0.4 fusion.92
  13.9 0.1 copy.24
  14.0 1.4 %multiply_reduce_fusion = f32[4,4,8,4,32]{4,3,2,1,0:T(4,128)S(1)} fusion(bf16[4,32,256,1,1,1]{2,1,0,5,4,3:T(8,128)(2,1)S(1)} %bitcast.148, f32[4,4,8,16,4]{3,4,2,1,0:T(4,128)S(1)} %get-tuple-element.8, bf16[4,4,8,16,256]{4,3,2,1,0:T(8,128)(2,1)S(1)} %copy-done.3, f32[16,256]{1,0:T(8,128)S(1)} %fusion.47), kind=kOutput, calls=%fused_computation | convolution fusion | flops 136298496 | bytes 1228800 | tf_op jit(solution)/shard_map/dot_general | solution.py:73
  15.4 0.0 copy-start
  15.4 0.2 copy.27
  15.6 0.7 %reshape.250 = f32[4,1,128]{2,1,0:T(1,128)} reshape(f32[4,4,4,8]{3,2,1,0:T(4,128)S(1)} %bitcast.145) | data formatting | bytes 4096
  16.2 0.8 %reshape.228 = f32[4,4,8,128]{3,2,1,0:T(8,128)} reshape(f32[4,4,8,4,32]{4,3,2,1,0:T(4,128)S(1)} %multiply_reduce_fusion) | data formatting | bytes 131072 | tf_op jit(solution)/shard_map/reshape | solution.py:82
  17.0 1.9 %all-to-all-done.1 = f32[4,1,128]{2,1,0:T(1,128)S(1)} async-done(((f32[4,1,128]{2,1,0:T(1,128)}), f32[4,1,128]{2,1,0:T(1,128)S(1)}, u32[]{:S(2)}, u32[]{:S(2)}) %all-to-all-start.1) | async-done | bytes 2080 | tf_op jit(solution)/shard_map/all_to_all | solution.py:84
  18.9 3.2 %all-to-all-start.2 = ((f32[4,1,128]{2,1,0:T(1,128)}), f32[4,1,128]{2,1,0:T(1,128)S(1)}, u32[]{:S(2)}, u32[]{:S(2)}) async-start(f32[4,1,128]{2,1,0:T(1,128)} %reshape.250), calls=%async_computation.2 | async-start | bytes 4096 | tf_op jit(solution)/shard_map/all_to_all | solution.py:85
  22.1 0.5 broadcast.137
  22.6 0.7 %reduce.6 = f32[4,128]{1,0:T(4,128)S(1)} reduce(f32[4,1,128]{2,1,0:T(1,128)S(1)} %all-to-all-done.1, f32[]{:T(128)} %broadcast.137), dimensions={1}, to_apply=%all_to_all.10.reduce_sub_computation | reduce | bytes 4100 | tf_op jit(solution)/shard_map/all_to_all | solution.py:84
  23.3 0.1 reshape.253
  23.4 4.1 %all-to-all-done.2 = f32[4,1,128]{2,1,0:T(1,128)S(1)} async-done(((f32[4,1,128]{2,1,0:T(1,128)}), f32[4,1,128]{2,1,0:T(1,128)S(1)}, u32[]{:S(2)}, u32[]{:S(2)}) %all-to-all-start.2) | async-done | bytes 2080 | tf_op jit(solution)/shard_map/all_to_all | solution.py:85
  27.5 3.3 %all-to-all-start = ((f32[4,4,8,128]{3,2,1,0:T(8,128)}), f32[4,4,8,128]{3,2,1,0:T(8,128)S(1)}, u32[]{:S(2)}, u32[]{:S(2)}) async-start(f32[4,4,8,128]{3,2,1,0:T(8,128)} %reshape.228), calls=%async_computation | async-start | bytes 131072 | tf_op jit(solution)/shard_map/all_to_all | solution.py:86
  30.8 0.7 %reduce.7 = f32[4,128]{1,0:T(4,128)S(1)} reduce(f32[4,1,128]{2,1,0:T(1,128)S(1)} %all-to-all-done.2, f32[]{:T(128)} %broadcast.137), dimensions={1}, to_apply=%all_to_all.11.reduce_sub_computation | reduce | bytes 4100 | tf_op jit(solution)/shard_map/all_to_all | solution.py:85
  31.5 0.1 reshape.251
  31.6 0.1 copy.28
  31.7 0.1 broadcast_in_dim.29
  31.8 0.1 broadcast_in_dim.30
  31.9 0.0 copy-start.1
  31.9 0.2 copy.26
  32.1 0.2 broadcast_in_dim.27
  32.3 0.2 broadcast_in_dim.28
  32.5 4.1 %all-to-all-done = f32[4,4,8,128]{3,2,1,0:T(8,128)S(1)} async-done(((f32[4,4,8,128]{3,2,1,0:T(8,128)}), f32[4,4,8,128]{3,2,1,0:T(8,128)S(1)}, u32[]{:S(2)}, u32[]{:S(2)}) %all-to-all-start) | async-done | bytes 65568 | tf_op jit(solution)/shard_map/all_to_all | solution.py:86
  36.5 1.3 %collective-permute-start.1 = (bf16[1,1,8,128]{3,2,1,0:T(8,128)(2,1)S(1)}, bf16[1,1,8,128]{3,2,1,0:T(8,128)(2,1)S(1)}, u32[]{:S(2)}, u32[]{:S(2)}) collective-permute-start(bf16[1,1,8,128]{3,2,1,0:T(8,128)(2,1)S(1)} %get-tuple-element.12), channel_id=1, source_target_pairs={{2,0},{3,1},{6,4},{7,5},{10,8},{11,9},{14,12},{15,13},{18,16},{19,... | collective-permute-start | bytes 6152 | tf_op jit(solution)/shard_map/ppermute | solution.py:21
  37.8 4.5 %collective-permute-start = (bf16[1,1,8,128]{3,2,1,0:T(8,128)(2,1)S(1)}, bf16[1,1,8,128]{3,2,1,0:T(8,128)(2,1)S(1)}, u32[]{:S(2)}, u32[]{:S(2)}) collective-permute-start(bf16[1,1,8,128]{3,2,1,0:T(8,128)(2,1)S(1)} %get-tuple-element.11), channel_id=1, source_target_pairs={{0,2},{1,3},{4,6},{5,7},{8,10},{9,11},{12,14},{13,15},{16,18},{17,... | collective-permute-start | bytes 6152 | tf_op jit(solution)/shard_map/ppermute | solution.py:18
  42.4 0.0 collective-permute-done.1
  42.4 1.3 %collective-permute-done = bf16[1,1,8,128]{3,2,1,0:T(8,128)(2,1)S(1)} collective-permute-done((bf16[1,1,8,128]{3,2,1,0:T(8,128)(2,1)S(1)}, bf16[1,1,8,128]{3,2,1,0:T(8,128)(2,1)S(1)}, u32[]{:S(2)}, u32[]{:S(2)}) %collective-permute-start) | collective-permute-done | bytes 2080 | tf_op jit(solution)/shard_map/ppermute | solution.py:18
  43.7 1.8 %all_gather.6 = bf16[1,6,8,256]{3,2,1,0:T(8,128)(2,1)S(1)} all-gather(bf16[1,6,8,128]{3,2,1,0:T(8,128)(2,1)S(1)} %pad_maximum_fusion), channel_id=1, replica_groups=mesh['groups'=2,'date'=4,'tile'=2,'head'=2] {'head'}, dimensions={3}, use_global_device_ids=true | all-gather | bytes 36864 | tf_op jit(solution)/shard_map/all_gather | solution.py:49
  45.5 0.1 fusion.27
  45.6 0.1 convolution_add_fusion.15
  45.8 0.1 convolution_add_fusion.14
  45.9 0.1 convolution_add_fusion.13
  46.0 0.1 convolution_add_fusion.12
  46.2 0.1 convolution_add_fusion.11
  46.3 0.1 convolution_add_fusion.10
  46.5 0.1 convolution_add_fusion.9
  46.6 0.1 fusion.4
  46.7 1.3 %collective-permute-start.3 = (bf16[1,1,8,128]{3,2,1,0:T(8,128)(2,1)S(1)}, bf16[1,1,8,128]{3,2,1,0:T(8,128)(2,1)S(1)}, u32[]{:S(2)}, u32[]{:S(2)}) collective-permute-start(bf16[1,1,8,128]{3,2,1,0:T(8,128)(2,1)S(1)} %get-tuple-element.10), channel_id=1, source_target_pairs={{2,0},{3,1},{6,4},{7,5},{10,8},{11,9},{14,12},{15,13},{18,16},{19,... | collective-permute-start | bytes 6152 | tf_op jit(solution)/shard_map/ppermute | solution.py:21
  48.0 4.5 %collective-permute-start.2 = (bf16[1,1,8,128]{3,2,1,0:T(8,128)(2,1)S(1)}, bf16[1,1,8,128]{3,2,1,0:T(8,128)(2,1)S(1)}, u32[]{:S(2)}, u32[]{:S(2)}) collective-permute-start(bf16[1,1,8,128]{3,2,1,0:T(8,128)(2,1)S(1)} %get-tuple-element.9), channel_id=1, source_target_pairs={{0,2},{1,3},{4,6},{5,7},{8,10},{9,11},{12,14},{13,15},{16,18},{17,... | collective-permute-start | bytes 6152 | tf_op jit(solution)/shard_map/ppermute | solution.py:18
  52.6 0.0 collective-permute-done.3
  52.6 1.3 %collective-permute-done.2 = bf16[1,1,8,128]{3,2,1,0:T(8,128)(2,1)S(1)} collective-permute-done((bf16[1,1,8,128]{3,2,1,0:T(8,128)(2,1)S(1)}, bf16[1,1,8,128]{3,2,1,0:T(8,128)(2,1)S(1)}, u32[]{:S(2)}, u32[]{:S(2)}) %collective-permute-start.2) | collective-permute-done | bytes 2080 | tf_op jit(solution)/shard_map/ppermute | solution.py:18
  53.9 1.8 %all_gather.7 = bf16[1,6,8,256]{3,2,1,0:T(8,128)(2,1)S(1)} all-gather(bf16[1,6,8,128]{3,2,1,0:T(8,128)(2,1)S(1)} %pad_maximum_fusion.1), channel_id=1, replica_groups=mesh['groups'=2,'date'=4,'tile'=2,'head'=2] {'head'}, dimensions={3}, use_global_device_ids=true | all-gather | bytes 36864 | tf_op jit(solution)/shard_map/all_gather | solution.py:49
  55.7 0.1 fusion.17
  55.8 0.1 convolution_add_fusion.7
  56.0 0.1 convolution_add_fusion.6
  56.1 0.1 convolution_add_fusion.5
  56.2 0.1 convolution_add_fusion.4
  56.4 0.1 convolution_add_fusion.3
  56.5 0.1 convolution_add_fusion.2
  56.7 0.1 convolution_add_fusion.1
  56.8 0.7 %fusion.3 = bf16[1,4,8,128]{3,2,1,0:T(8,128)(2,1)} fusion(f32[32,128]{1,0:T(8,128)S(1)} %convolution_add_fusion.1, bf16[3,3,256,128]{3,2,1,0:T(8,128)(2,1)S(1)} %copy-done.1, bf16[1,6,8,256]{3,2,1,0:T(8,128)(2,1)S(1)} %all_gather.7), kind=kOutput, calls=%fused_computation.22 | convolution fusion | flops 2105344 | bytes 114688 | tf_op jit(solution)/shard_map/dot_general | solution.py:55
  (14 shorter events, 0.1 us)
Async XLA Ops:
  6.0 7.8 %copy-start.2 = (bf16[256,128]{1,0:T(8,128)(2,1)S(1)}, bf16[256,128]{1,0:T(8,128)(2,1)}, u32[]{:S(2)}) copy-start(bf16[256,128]{1,0:T(8,128)(2,1)} %param.13) | copy-start | bytes 196612
  6.0 7.9 %copy-start.3 = (bf16[4,4,8,16,256]{4,3,2,1,0:T(8,128)(2,1)S(1)}, bf16[4,4,8,16,256]{4,3,2,1,0:T(8,128)(2,1)}, u32[]{:S(2)}) copy-start(bf16[4,4,8,16,256]{4,3,2,1,0:T(8,128)(2,1)} %param.8) | copy-start | bytes 3145732
  7.1 11.8 %all-to-all-start.1 = ((f32[4,1,128]{2,1,0:T(1,128)}), f32[4,1,128]{2,1,0:T(1,128)S(1)}, u32[]{:S(2)}, u32[]{:S(2)}) async-start(f32[4,1,128]{2,1,0:T(1,128)} %reshape.252), calls=%async_computation.1 | async-start | bytes 4096 | tf_op jit(solution)/shard_map/all_to_all | solution.py:84
  15.4 30.1 %copy-start = (bf16[3,3,256,128]{3,2,1,0:T(8,128)(2,1)S(1)}, bf16[3,3,256,128]{3,2,1,0:T(8,128)(2,1)}, u32[]{:S(2)}) copy-start(bf16[3,3,256,128]{3,2,1,0:T(8,128)(2,1)} %param.14) | copy-start | bytes 1769476
  18.9 8.6 %all-to-all-start.2 = ((f32[4,1,128]{2,1,0:T(1,128)}), f32[4,1,128]{2,1,0:T(1,128)S(1)}, u32[]{:S(2)}, u32[]{:S(2)}) async-start(f32[4,1,128]{2,1,0:T(1,128)} %reshape.250), calls=%async_computation.2 | async-start | bytes 4096 | tf_op jit(solution)/shard_map/all_to_all | solution.py:85
  27.5 9.0 %all-to-all-start = ((f32[4,4,8,128]{3,2,1,0:T(8,128)}), f32[4,4,8,128]{3,2,1,0:T(8,128)S(1)}, u32[]{:S(2)}, u32[]{:S(2)}) async-start(f32[4,4,8,128]{3,2,1,0:T(8,128)} %reshape.228), calls=%async_computation | async-start | bytes 131072 | tf_op jit(solution)/shard_map/all_to_all | solution.py:86
  31.9 23.8 %copy-start.1 = (bf16[3,3,256,128]{3,2,1,0:T(8,128)(2,1)S(1)}, bf16[3,3,256,128]{3,2,1,0:T(8,128)(2,1)}, u32[]{:S(2)}) copy-start(bf16[3,3,256,128]{3,2,1,0:T(8,128)(2,1)} %param.15) | copy-start | bytes 1769476
  36.5 5.9 %collective-permute-start.1 = (bf16[1,1,8,128]{3,2,1,0:T(8,128)(2,1)S(1)}, bf16[1,1,8,128]{3,2,1,0:T(8,128)(2,1)S(1)}, u32[]{:S(2)}, u32[]{:S(2)}) collective-permute-start(bf16[1,1,8,128]{3,2,1,0:T(8,128)(2,1)S(1)} %get-tuple-element.12), channel_id=1, source_target_pairs={{2,0},{3,1},{6,4},{7,5},{10,8},{11,9},{14,12},{15,13},{18,16},{19,... | collective-permute-start | bytes 6152 | tf_op jit(solution)/shard_map/ppermute | solution.py:21
  37.8 5.8 %collective-permute-start = (bf16[1,1,8,128]{3,2,1,0:T(8,128)(2,1)S(1)}, bf16[1,1,8,128]{3,2,1,0:T(8,128)(2,1)S(1)}, u32[]{:S(2)}, u32[]{:S(2)}) collective-permute-start(bf16[1,1,8,128]{3,2,1,0:T(8,128)(2,1)S(1)} %get-tuple-element.11), channel_id=1, source_target_pairs={{0,2},{1,3},{4,6},{5,7},{8,10},{9,11},{12,14},{13,15},{16,18},{17,... | collective-permute-start | bytes 6152 | tf_op jit(solution)/shard_map/ppermute | solution.py:18
  46.7 5.9 %collective-permute-start.3 = (bf16[1,1,8,128]{3,2,1,0:T(8,128)(2,1)S(1)}, bf16[1,1,8,128]{3,2,1,0:T(8,128)(2,1)S(1)}, u32[]{:S(2)}, u32[]{:S(2)}) collective-permute-start(bf16[1,1,8,128]{3,2,1,0:T(8,128)(2,1)S(1)} %get-tuple-element.10), channel_id=1, source_target_pairs={{2,0},{3,1},{6,4},{7,5},{10,8},{11,9},{14,12},{15,13},{18,16},{19,... | collective-permute-start | bytes 6152 | tf_op jit(solution)/shard_map/ppermute | solution.py:21
  48.0 5.8 %collective-permute-start.2 = (bf16[1,1,8,128]{3,2,1,0:T(8,128)(2,1)S(1)}, bf16[1,1,8,128]{3,2,1,0:T(8,128)(2,1)S(1)}, u32[]{:S(2)}, u32[]{:S(2)}) collective-permute-start(bf16[1,1,8,128]{3,2,1,0:T(8,128)(2,1)S(1)} %get-tuple-element.9), channel_id=1, source_target_pairs={{0,2},{1,3},{4,6},{5,7},{8,10},{9,11},{12,14},{13,15},{16,18},{17,... | collective-permute-start | bytes 6152 | tf_op jit(solution)/shard_map/ppermute | solution.py:18
where the time goes:
time: 58.1 us; the launch traced here: 57.5 us
  starting transfers between devices  24.5 us (42%)
  waiting for transfers between devices  12.6 us (22%)
  matrix products  7.09 us (12%)
  local copies, waits for them, and re-layouts  5.82 us (10%)
  other arithmetic  3.7 us (6%)
  blocking collectives  3.62 us (6%)
    ppermute x2, starting transfers between devices, with_halo(): lax.ppermute(lax.slice_in_dim(block, block.shape[dim] - width, None, axis...  9.08 us
    all_to_all x1, starting transfers between devices, local(): lax.all_to_all(top, 'date', split_axis=0, concat_axis=0, tiled=True)  6.32 us
    all_to_all x1, waiting for transfers between devices, local(): lax.all_to_all(totals, 'date', split_axis=0, concat_axis=0, tiled=True)  4.08 us
    all_to_all x1, waiting for transfers between devices, local(): lax.all_to_all(sums, 'date', split_axis=0, concat_axis=0, tiled=True)  4.05 us
    all_gather x2, blocking collectives, convolve(): whole = lax.all_gather(padded, 'head', axis=3, tiled=True)  3.62 us
    all_to_all x1, starting transfers between devices, local(): lax.all_to_all(sums, 'date', split_axis=0, concat_axis=0, tiled=True)  3.28 us
    all_to_all x1, starting transfers between devices, local(): lax.all_to_all(totals, 'date', split_axis=0, concat_axis=0, tiled=True)  3.2 us
    dot_general x18, matrix products, convolve(): jnp.dot(piece, kernel[arow, bcol], preferred_element_type=jnp.float32)  3.05 us
  transfers between devices with their start and end apart: 7, of which 5 were waited for; matrix products, arithmetic and copies ran while one was open for 11% of the time, Pallas kernels for 0%

commit v1 on v0

v1 whole, which is shorter than its diff:
```python
import functools
import math

import jax
import jax.numpy as jnp
from jax import lax
from jax.experimental import pallas as pl
from jax.experimental.pallas import tpu as pltpu
from jax.sharding import PartitionSpec as P

HSIZE = 32
HALO = 2
MESH = pl.DeviceIdType.MESH
F32, BF16 = jnp.float32, jnp.bfloat16


cloud_penalty = 6.0


def iota(shape, dim):
    return lax.broadcasted_iota(jnp.int32, shape, dim)


def frequencies(width):
    pair = iota((1, width), 1) // 2
    freq = jnp.ones((1, width), F32)
    bit = 1
    while bit < width // 2:
        freq = jnp.where((pair // bit) % 2 == 1, freq * F32(1000.0 ** (-2.0 * bit / width)), freq)
        bit *= 2
    return freq


def encoding(days, width):
    angle = days * frequencies(width)
    turns = jnp.floor(angle * F32(2.0 / math.pi) + F32(0.5))
    rest = angle - turns * F32(1.5703125)
    rest = rest - turns * F32(4.837512969970703125e-4)
    rest = rest - turns * F32(7.54978995489188216e-8)
    square = rest * rest
    sine = (F32(-1.9515295891e-4) * square + F32(8.3321608736e-3)) * square + F32(-1.6666654611e-1)
    sine = sine * square * rest + rest
    cosine = (F32(2.443315711809948e-5) * square + F32(-1.388731625493765e-3)) * square
    cosine = (cosine + F32(4.166664568298827e-2)) * square * square - F32(0.5) * square + F32(1.0)
    quadrant = turns.astype(jnp.int32) + iota(angle.shape, 1) % 2
    value = jnp.where(quadrant % 2 == 1, cosine, sine)
    return jnp.where((quadrant // 2) % 2 == 1, -value, value)


def split(value, parts):
    terms = []
    for _ in range(parts):
        term = value.astype(BF16)
        terms.append(term)
        value = value - term.astype(F32)
    return terms


def shifted(field, cols):
    count = field.shape[0]
    col = iota(field.shape, 0) % cols
    left = jnp.where(col == 0, 0.0, pltpu.roll(field, 1, 0))
    right = jnp.where(col == cols - 1, 0.0, pltpu.roll(field, count - 1, 0))
    return left, field, right


def windows(field, cols):
    sides = shifted(field, cols)
    count = field.shape[0] - 2 * cols
    return jnp.concatenate(
        [side[arow * cols : arow * cols + count].astype(BF16) for arow in range(3) for side in sides],
        axis=1,
    )


def kernel(
    sizes,
    tokens,
    mask,
    days,
    query,
    key_weight,
    value_weight,
    conv_first,
    conv_second,
    out,
    tok_v,
    mask_v,
    wk_v,
    wv_v,
    w1_v,
    w2_v,
    proj_v,
    enc_v,
    part_s,
    part_r,
    pool_v,
    tok_sem,
    in_sem,
    w1_send,
    w1_recv,
    part_send,
    part_recv,
    pool_send,
    pool_recv,
):
    n, slabs, rows, cols, dates, width = sizes
    pixels = rows * cols
    chans = query.shape[1]
    date, slab, head = lax.axis_index("date"), lax.axis_index("tile"), lax.axis_index("head")
    other = 1 - head
    has_up, has_down = slab > 0, slab < slabs - 1

    def tile_at(step):
        return lax.rem(date + 1 + step, n)

    def tok_copy(tile):
        return pltpu.make_async_copy(tokens.at[tile], tok_v.at[tile], tok_sem.at[tile])

    loads = [
        pltpu.make_async_copy(key_weight, wk_v, in_sem.at[0]),
        pltpu.make_async_copy(value_weight, wv_v, in_sem.at[1]),
        pltpu.make_async_copy(mask, mask_v, in_sem.at[2]),
        pltpu.make_async_copy(conv_first, w1_v.at[head], in_sem.at[3]),
        pltpu.make_async_copy(conv_second, w2_v, in_sem.at[4]),
    ]
    for load in loads[:3]:
        load.start()

    @pl.loop(0, n)
    def _(step):
        tok_copy(tile_at(step)).start()

    for load in loads[3:]:
        load.start()

    barrier = pltpu.get_barrier_semaphore()

    @pl.loop(1, n)
    def _(step):
        pl.semaphore_signal(barrier, inc=1, device_id={"date": lax.rem(date + step, n)}, device_id_type=MESH)

    pl.semaphore_signal(barrier, inc=1, device_id={"head": other}, device_id_type=MESH)
    for has, off in ((has_up, -1), (has_down, 1)):

        @pl.when(has)
        def _(off=off):
            for core in range(2):
                pl.semaphore_signal(
                    barrier, inc=1, device_id={"tile": slab + off, "head": core}, device_id_type=MESH
                )

    day_row = days[...].astype(F32)
    eye = iota((dates, dates), 0) == iota((dates, dates), 1)
    day_col = jnp.sum(jnp.where(eye, jnp.broadcast_to(day_row, (dates, dates)), 0.0), axis=1, keepdims=True)
    enc_v[...] = encoding(day_col, width)

    same_head = iota((chans, chans), 0) // HSIZE == iota((chans, chans), 1) // HSIZE
    blocks = jnp.where(same_head, 1.0, 0.0).astype(BF16)
    loads[0].wait()
    loads[1].wait()
    scaled = wk_v[...].astype(F32) * (query[...] * F32(1.0 / math.sqrt(HSIZE)))
    folded = jnp.zeros((width, chans), F32)
    for term in split(scaled, 3):
        folded = folded + jnp.dot(term, blocks, preferred_element_type=F32)
    high, low = split(folded, 2)
    proj_v[:, :chans] = wv_v[...]
    proj_v[:, chans : 2 * chans] = high
    proj_v[:, 2 * chans :] = low
    loads[2].wait()

    has_count = has_up.astype(jnp.int32) + has_down.astype(jnp.int32)
    pl.semaphore_wait(barrier, n + 2 * has_count)

    w1_copy = pltpu.make_async_remote_copy(
        src_ref=conv_first,
        dst_ref=w1_v.at[head],
        send_sem=w1_send,
        recv_sem=w1_recv,
        device_id={"head": other},
        device_id_type=MESH,
    )
    w1_copy.start()

    lane = iota((8, chans), 1) % HSIZE // 4
    ones = jnp.ones((dates, chans), BF16)

    def part_copy(tile, slot):
        return pltpu.make_async_remote_copy(
            src_ref=part_s.at[tile],
            dst_ref=part_r.at[slot],
            send_sem=part_send.at[tile],
            recv_sem=part_recv.at[slot],
            device_id={"date": tile},
            device_id_type=MESH,
        )

    def attend(tile):
        feats = tok_v[tile].astype(F32).reshape(pixels, dates, width)
        inputs = (feats + enc_v[...][None]).astype(BF16).reshape(pixels * dates, width)
        both = jnp.dot(inputs, proj_v[...], preferred_element_type=F32)
        clear = jnp.broadcast_to(mask_v[tile].astype(F32)[:, None, :], (pixels, dates, dates))
        cloud = jnp.where(eye[None], F32(-cloud_penalty) * (1.0 - clear), 0.0).astype(BF16)
        cloud = jnp.dot(cloud.reshape(pixels * dates, dates), ones, preferred_element_type=F32)
        score = both[:, chans : 2 * chans] + both[:, 2 * chans :] + cloud
        score = score.reshape(pixels, dates, chans)
        vals = both[:, :chans].reshape(pixels, dates, chans)
        top = jnp.max(score, axis=1)
        expo = jnp.exp(score - top[:, None, :])
        total = jnp.sum(expo, axis=1)
        sums = jnp.sum(expo * vals, axis=1)
        groups = pixels // 8
        stats = top[:8]
        for group in range(groups):
            stats = jnp.where(lane == group, top[group * 8 : group * 8 + 8], stats)
            stats = jnp.where(lane == group + groups, total[group * 8 : group * 8 + 8], stats)
        return sums, stats

    @pl.loop(0, n - 1)
    def _(step):
        tile = tile_at(step)
        tok_copy(tile).wait()
        sums, stats = attend(tile)
        part_s[tile, :pixels] = sums
        part_s[tile, pixels:] = stats
        part_copy(tile, date).start()

    tok_copy(date).wait()
    sums, stats = attend(date)
    part_r[date, :pixels] = sums
    part_r[date, pixels:] = stats

    @pl.loop(1, n)
    def _(step):
        part_copy(date, lax.rem(date + step, n)).wait_recv()

    best = part_r[0, pixels:]
    for source in range(1, n):
        best = jnp.maximum(best, part_r[source, pixels:])
    scales = []
    tots = jnp.zeros((8, chans), F32)
    for source in range(n):
        stat = part_r[source, pixels:]
        scale = jnp.exp(stat - best)
        scales.append(scale)
        tots = tots + scale * pltpu.roll(stat, chans - HSIZE // 2, 1)
    inverse = 1.0 / tots
    groups = pixels // 8
    pooled = [jnp.zeros((8, chans), F32) for _ in range(groups)]
    for source in range(n):
        weight = scales[source] * inverse
        for group in range(groups):
            wide = weight if group == 0 else pltpu.roll(weight, chans - 4 * group, 1)
            wide = jnp.where(lane == 0, wide, 0.0)
            for step in (4, 8, 16):
                wide = wide + pltpu.roll(wide, step, 1)
            pooled[group] = pooled[group] + wide * part_r[source, group * 8 : group * 8 + 8]
    halo = HALO * cols
    pool_v[head, halo : halo + pixels] = jnp.concatenate(pooled, axis=0).astype(BF16)

    def pool_copy(index, source, target, count, where):
        return pltpu.make_async_remote_copy(
            src_ref=pool_v.at[head, pl.ds(source, count)],
            dst_ref=pool_v.at[head, pl.ds(target, count)],
            send_sem=pool_send.at[index],
            recv_sem=pool_recv.at[index],
            device_id=where,
            device_id_type=MESH,
        )

    def sends(fn):
        fn(pool_copy(0, halo, halo, pixels, {"head": other}))

        @pl.when(has_up)
        def _():
            for hop in range(2):
                core = other if hop == 0 else head
                fn(pool_copy(1 + hop, halo, halo + pixels, halo, {"tile": slab - 1, "head": core}))

        @pl.when(has_down)
        def _():
            for hop in range(2):
                core = other if hop == 0 else head
                fn(pool_copy(3 + hop, pixels, 0, halo, {"tile": slab + 1, "head": core}))

    sends(lambda copy: copy.start())

    zeros = jnp.zeros((2, halo, chans), BF16)

    @pl.when(jnp.logical_not(has_up))
    def _():
        pool_v[:, :halo] = zeros

    @pl.when(jnp.logical_not(has_down))
    def _():
        pool_v[:, halo + pixels :] = zeros

    for load in loads[3:]:
        load.wait()
    w1_copy.wait()

    pool_copy(0, halo, halo, pixels, {"head": other}).wait_recv()

    @pl.when(has_down)
    def _():
        for hop in range(2):
            pool_copy(1 + hop, halo, halo + pixels, halo, {"head": other}).wait_recv()

    @pl.when(has_up)
    def _():
        for hop in range(2):
            pool_copy(3 + hop, pixels, 0, halo, {"head": other}).wait_recv()

    field = jnp.concatenate([pool_v[0], pool_v[1]], axis=1).astype(F32)
    first = jnp.concatenate([w1_v[0], w1_v[1]], axis=1)
    hidden = jnp.dot(windows(field, cols), first, preferred_element_type=F32)
    hidden = jnp.maximum(hidden, 0.0).astype(BF16).astype(F32)
    place = iota(hidden.shape, 0) // cols + (slab * rows - 1)
    hidden = jnp.where((place >= 0) & (place < slabs * rows), hidden, 0.0)
    out[...] = jnp.dot(windows(hidden, cols), w2_v[...], preferred_element_type=F32).astype(BF16)

    @pl.loop(0, n - 1)
    def _(step):
        part_copy(tile_at(step), date).wait_send()

    sends(lambda copy: copy.wait_send())


def local(n, slabs, tokens, cloud_mask, day_of_year, query, key_weight, value_weight, conv_first, conv_second):
    tiles, rows, cols, dates, width = tokens.shape
    pixels = rows * cols
    chans = query.shape[0]
    depth = 9 * width
    anywhere = pl.BlockSpec(memory_space=pl.ANY)
    vmem = pl.BlockSpec(memory_space=pltpu.VMEM)
    result = pl.pallas_call(
        functools.partial(kernel, (n, slabs, rows, cols, dates, width)),
        out_shape=jax.ShapeDtypeStruct((pixels, chans), BF16),
        in_specs=[anywhere, anywhere, vmem, vmem] + [anywhere] * 4,
        out_specs=vmem,
        scratch_shapes=[
            pltpu.VMEM((n, pixels * dates, width), BF16),
            pltpu.VMEM((n, pixels, dates), jnp.int32),
            pltpu.VMEM((width, chans), BF16),
            pltpu.VMEM((width, chans), BF16),
            pltpu.VMEM((2, depth, chans), BF16),
            pltpu.VMEM((depth, chans), BF16),
            pltpu.VMEM((width, 3 * chans), BF16),
            pltpu.VMEM((dates, width), F32),
            pltpu.VMEM((n, pixels + 8, chans), F32),
            pltpu.VMEM((n, pixels + 8, chans), F32),
            pltpu.VMEM((2, pixels + 2 * HALO * cols, chans), BF16),
            pltpu.SemaphoreType.DMA((n,)),
            pltpu.SemaphoreType.DMA((5,)),
            pltpu.SemaphoreType.DMA,
            pltpu.SemaphoreType.DMA,
            pltpu.SemaphoreType.DMA((n,)),
            pltpu.SemaphoreType.DMA((n,)),
            pltpu.SemaphoreType.DMA((5,)),
            pltpu.SemaphoreType.DMA((5,)),
        ],
        compiler_params=pltpu.CompilerParams(
            collective_id=0, has_side_effects=True, vmem_limit_bytes=48 * 1024 * 1024
        ),
    )(
        tokens.reshape(tiles, pixels * dates, width),
        cloud_mask.reshape(tiles, pixels, dates),
        day_of_year.reshape(1, dates),
        query.reshape(1, chans),
        key_weight,
        value_weight,
        conv_first.reshape(depth, chans),
        conv_second.reshape(depth, chans),
    )
    return result.reshape(1, rows, cols, chans)


def solution(mesh):
    in_specs = (
        P("groups", "tile", None, "date", None),
        P("groups", "tile", None, "date"),
        P(("groups", "date")),
        P("head"),
        P(None, "head"),
        P(None, "head"),
        P(None, None, None, "head"),
        P(None, None, None, "head"),
    )
    out_specs = P(("groups", "date"), "tile", None, "head")
    body = functools.partial(local, mesh.shape["date"], mesh.shape["tile"])
    return jax.shard_map(body, mesh=mesh, in_specs=in_specs, out_specs=out_specs, check_vma=False)
```

time: 58.1 us -> 21.3 us (0.37)
  starting transfers between devices: 24.5 us -> 0 us
  Pallas kernels: 0 us -> 13.8 us
  waiting for transfers between devices: 12.6 us -> 0 us
  matrix products: 7.09 us -> 0 us
  other arithmetic: 3.7 us -> 0 us
  blocking collectives: 3.62 us -> 0 us
  local copies, waits for them, and re-layouts: 5.82 us -> 7.14 us
    pallas_call x0 -> x1, Pallas kernels: none -> 13.8 us  [local(): pl.pallas_call(functools.partial(kernel, (n, slabs, rows, cols, dates, wi...]
    all_to_all x3 -> x0, starting transfers between devices: 12.8 us -> none  [the longest x1 6.32 us: local(): lax.all_to_all(top, 'date', split_axis=0, concat_axis=0, tiled=True)]
    ppermute x4 -> x0, starting transfers between devices: 11.7 us -> none  [the longest x2 9.08 us: with_halo(): lax.ppermute(lax.slice_in_dim(block, block.shape[dim] - width, None, axis...]
    all_to_all x3 -> x0, waiting for transfers between devices: 10 us -> none  [the longest x1 4.08 us: local(): lax.all_to_all(totals, 'date', split_axis=0, concat_axis=0, tiled=True)]
    dot_general x20 -> x0, matrix products: 7.09 us -> none  [the longest x18 3.05 us: convolve(): jnp.dot(piece, kernel[arow, bcol], preferred_element_type=jnp.float32)]
    unnamed x14 -> x17, local copies, waits for them, and re-layouts: 2.64 us -> 7.14 us
    all_gather x2 -> x0, blocking collectives: 3.62 us -> none  [convolve(): whole = lax.all_gather(padded, 'head', axis=3, tiled=True)]
    ppermute x4 -> x0, waiting for transfers between devices: 2.57 us -> none  [the longest x2 2.56 us: with_halo(): lax.ppermute(lax.slice_in_dim(block, block.shape[dim] - width, None, axis...]
  transfers between devices with their start and end apart: 7 -> 0, of which waited for: 5 -> 0; matrix products, arithmetic and copies ran while one was open for 11% -> 0% of each run, Pallas kernels for 0% -> 0%
where the time goes in v1:
time: 21.3 us; the launch traced here: 20.9 us
  Pallas kernels  13.8 us (65%)
  local copies, waits for them, and re-layouts  7.14 us (34%)
    pallas_call x1, Pallas kernels, local(): pl.pallas_call(functools.partial(kernel, (n, slabs, rows, cols, dates, wi...  13.8 us
    unnamed x17, local copies, waits for them, and re-layouts  7.14 us

profile of v1, /device:TPU:0, one launch (start us, length us, event | category | flops | bytes accessed | tf_op | source)
XLA Modules:
  0.0 20.9 jit_solution(15819819839038626674)
XLA Ops:
  0.0 0.0 copy-start.6
  0.0 0.0 copy-start.7
  0.0 0.7 %copy-done.6 = s32[16]{0:T(128)S(1)} copy-done((s32[16]{0:T(128)S(1)}, s32[16]{0:T(128)}, u32[]{:S(2)}) %copy-start.6) | copy-done | bytes 88
  0.7 0.0 copy-done.7
  0.7 0.0 copy-start
  0.7 1.2 %copy-done = bf16[4,4,8,16,256]{4,3,2,1,0:T(8,128)(2,1)S(1)} copy-done((bf16[4,4,8,16,256]{4,3,2,1,0:T(8,128)(2,1)S(1)}, bf16[4,4,8,16,256]{4,3,2,1,0:T(8,128)(2,1)}, u32[]{:S(2)}) %copy-start) | copy-done | bytes 1048600
  1.9 0.0 copy-start.1
  1.9 1.1 %copy-done.1 = bf16[3,3,256,128]{3,2,1,0:T(8,128)(2,1)S(1)} copy-done((bf16[3,3,256,128]{3,2,1,0:T(8,128)(2,1)S(1)}, bf16[3,3,256,128]{3,2,1,0:T(8,128)(2,1)}, u32[]{:S(2)}) %copy-start.1) | copy-done | bytes 589848
  3.0 0.0 copy-start.2
  3.0 1.1 %copy-done.2 = bf16[3,3,256,128]{3,2,1,0:T(8,128)(2,1)S(1)} copy-done((bf16[3,3,256,128]{3,2,1,0:T(8,128)(2,1)S(1)}, bf16[3,3,256,128]{3,2,1,0:T(8,128)(2,1)}, u32[]{:S(2)}) %copy-start.2) | copy-done | bytes 589848
  4.0 0.0 copy-start.3
  4.0 0.8 %copy-done.3 = s32[4,4,8,16]{3,2,1,0:T(8,128)S(1)} copy-done((s32[4,4,8,16]{3,2,1,0:T(8,128)S(1)}, s32[4,4,8,16]{3,2,1,0:T(8,128)}, u32[]{:S(2)}) %copy-start.3) | copy-done | bytes 8216
  4.9 0.0 copy-start.4
  4.9 0.8 %copy-done.4 = bf16[256,128]{1,0:T(8,128)(2,1)S(1)} copy-done((bf16[256,128]{1,0:T(8,128)(2,1)S(1)}, bf16[256,128]{1,0:T(8,128)(2,1)}, u32[]{:S(2)}) %copy-start.4) | copy-done | bytes 65560
  5.7 0.0 copy-start.5
  5.7 0.8 %copy-done.5 = bf16[256,128]{1,0:T(8,128)(2,1)S(1)} copy-done((bf16[256,128]{1,0:T(8,128)(2,1)S(1)}, bf16[256,128]{1,0:T(8,128)(2,1)}, u32[]{:S(2)}) %copy-start.5) | copy-done | bytes 65560
  6.5 13.8 %shard_map.82 = bf16[32,128]{1,0:T(8,128)(2,1)S(1)} custom-call(bf16[4,512,256]{2,1,0:T(8,128)(2,1)S(1)} %bitcast.7, s32[4,32,16]{2,1,0:T(8,128)S(1)} %bitcast.10, s32[1,16]{1,0:T(1,128)S(1)} %bitcast.12, f32[1,128]{1,0:T(1,128)S(1)} %bitcast.13, bf16[256,128]{1,0:T(8,128)(2,1)S(1)} %copy-done.4, bf16[256,128]{1,0:T(8,128)(2,1)S(1)} %copy-done.5, ...), custom_call_target="tpu_custom_call" | custom-call | tf_op jit(solution)/shard_map/pallas_call | solution.py:336
  20.3 0.6 %copy.10 = bf16[1,4,8,128]{3,2,1,0:T(8,128)(2,1)} copy(bf16[1,4,8,128]{3,2,1,0:T(8,128)(2,1)S(1)} %bitcast.11) | data formatting | bytes 16384
Async XLA Ops:
  0.0 0.7 %copy-start.6 = (s32[16]{0:T(128)S(1)}, s32[16]{0:T(128)}, u32[]{:S(2)}) copy-start(s32[16]{0:T(128)} %param.10) | copy-start | bytes 196
  0.0 0.7 %copy-start.7 = (f32[128]{0:T(128)S(1)}, f32[128]{0:T(128)}, u32[]{:S(2)}) copy-start(f32[128]{0:T(128)} %param.11) | copy-start | bytes 1540
  0.7 1.2 %copy-start = (bf16[4,4,8,16,256]{4,3,2,1,0:T(8,128)(2,1)S(1)}, bf16[4,4,8,16,256]{4,3,2,1,0:T(8,128)(2,1)}, u32[]{:S(2)}) copy-start(bf16[4,4,8,16,256]{4,3,2,1,0:T(8,128)(2,1)} %param.8) | copy-start | bytes 3145732
  1.9 1.1 %copy-start.1 = (bf16[3,3,256,128]{3,2,1,0:T(8,128)(2,1)S(1)}, bf16[3,3,256,128]{3,2,1,0:T(8,128)(2,1)}, u32[]{:S(2)}) copy-start(bf16[3,3,256,128]{3,2,1,0:T(8,128)(2,1)} %param.14) | copy-start | bytes 1769476
  3.0 1.1 %copy-start.2 = (bf16[3,3,256,128]{3,2,1,0:T(8,128)(2,1)S(1)}, bf16[3,3,256,128]{3,2,1,0:T(8,128)(2,1)}, u32[]{:S(2)}) copy-start(bf16[3,3,256,128]{3,2,1,0:T(8,128)(2,1)} %param.15) | copy-start | bytes 1769476
  4.0 0.8 %copy-start.3 = (s32[4,4,8,16]{3,2,1,0:T(8,128)S(1)}, s32[4,4,8,16]{3,2,1,0:T(8,128)}, u32[]{:S(2)}) copy-start(s32[4,4,8,16]{3,2,1,0:T(8,128)} %param.9) | copy-start | bytes 24580
  4.9 0.8 %copy-start.4 = (bf16[256,128]{1,0:T(8,128)(2,1)S(1)}, bf16[256,128]{1,0:T(8,128)(2,1)}, u32[]{:S(2)}) copy-start(bf16[256,128]{1,0:T(8,128)(2,1)} %key_weight.1) | copy-start | bytes 196612
  5.7 0.8 %copy-start.5 = (bf16[256,128]{1,0:T(8,128)(2,1)S(1)}, bf16[256,128]{1,0:T(8,128)(2,1)}, u32[]{:S(2)}) copy-start(bf16[256,128]{1,0:T(8,128)(2,1)} %value_weight.1) | copy-start | bytes 196612

commit v2 on v1

--- a/solution.py
+++ b/solution.py
@@ -86,6 +86,8 @@
     out,
     tok_v,
     mask_v,
+    days_v,
+    query_v,
     wk_v,
     wv_v,
     w1_v,
@@ -118,20 +120,22 @@
         return pltpu.make_async_copy(tokens.at[tile], tok_v.at[tile], tok_sem.at[tile])
 
     loads = [
-        pltpu.make_async_copy(key_weight, wk_v, in_sem.at[0]),
-        pltpu.make_async_copy(value_weight, wv_v, in_sem.at[1]),
-        pltpu.make_async_copy(mask, mask_v, in_sem.at[2]),
-        pltpu.make_async_copy(conv_first, w1_v.at[head], in_sem.at[3]),
-        pltpu.make_async_copy(conv_second, w2_v, in_sem.at[4]),
+        pltpu.make_async_copy(days, days_v, in_sem.at[0]),
+        pltpu.make_async_copy(query, query_v, in_sem.at[1]),
+        pltpu.make_async_copy(key_weight, wk_v, in_sem.at[2]),
+        pltpu.make_async_copy(value_weight, wv_v, in_sem.at[3]),
+        pltpu.make_async_copy(mask, mask_v, in_sem.at[4]),
+        pltpu.make_async_copy(conv_first, w1_v.at[head], in_sem.at[5]),
+        pltpu.make_async_copy(conv_second, w2_v, in_sem.at[6]),
     ]
-    for load in loads[:3]:
+    for load in loads[:5]:
         load.start()
 
     @pl.loop(0, n)
     def _(step):
         tok_copy(tile_at(step)).start()
 
-    for load in loads[3:]:
+    for load in loads[5:]:
         load.start()
 
     barrier = pltpu.get_barrier_semaphore()
@@ -150,16 +154,17 @@
                     barrier, inc=1, device_id={"tile": slab + off, "head": core}, device_id_type=MESH
                 )
 
-    day_row = days[...].astype(F32)
+    loads[0].wait()
+    day_row = days_v[...].astype(F32)
     eye = iota((dates, dates), 0) == iota((dates, dates), 1)
     day_col = jnp.sum(jnp.where(eye, jnp.broadcast_to(day_row, (dates, dates)), 0.0), axis=1, keepdims=True)
     enc_v[...] = encoding(day_col, width)
 
     same_head = iota((chans, chans), 0) // HSIZE == iota((chans, chans), 1) // HSIZE
     blocks = jnp.where(same_head, 1.0, 0.0).astype(BF16)
-    loads[0].wait()
-    loads[1].wait()
-    scaled = wk_v[...].astype(F32) * (query[...] * F32(1.0 / math.sqrt(HSIZE)))
+    for load in loads[1:4]:
+        load.wait()
+    scaled = wk_v[...].astype(F32) * (query_v[...] * F32(1.0 / math.sqrt(HSIZE)))
     folded = jnp.zeros((width, chans), F32)
     for term in split(scaled, 3):
         folded = folded + jnp.dot(term, blocks, preferred_element_type=F32)
@@ -167,7 +172,7 @@
     proj_v[:, :chans] = wv_v[...]
     proj_v[:, chans : 2 * chans] = high
     proj_v[:, 2 * chans :] = low
-    loads[2].wait()
+    loads[4].wait()
 
     has_count = has_up.astype(jnp.int32) + has_down.astype(jnp.int32)
     pl.semaphore_wait(barrier, n + 2 * has_count)
@@ -295,7 +300,7 @@
     def _():
         pool_v[:, halo + pixels :] = zeros
 
-    for load in loads[3:]:
+    for load in loads[5:]:
         load.wait()
     w1_copy.wait()
 
@@ -331,16 +336,18 @@
     pixels = rows * cols
     chans = query.shape[0]
     depth = 9 * width
-    anywhere = pl.BlockSpec(memory_space=pl.ANY)
+    hbm = pl.BlockSpec(memory_space=pltpu.HBM)
     vmem = pl.BlockSpec(memory_space=pltpu.VMEM)
     result = pl.pallas_call(
         functools.partial(kernel, (n, slabs, rows, cols, dates, width)),
         out_shape=jax.ShapeDtypeStruct((pixels, chans), BF16),
-        in_specs=[anywhere, anywhere, vmem, vmem] + [anywhere] * 4,
+        in_specs=[hbm] * 8,
         out_specs=vmem,
         scratch_shapes=[
             pltpu.VMEM((n, pixels * dates, width), BF16),
             pltpu.VMEM((n, pixels, dates), jnp.int32),
+            pltpu.VMEM((1, dates), jnp.int32),
+            pltpu.VMEM((1, chans), F32),
             pltpu.VMEM((width, chans), BF16),
             pltpu.VMEM((width, chans), BF16),
             pltpu.VMEM((2, depth, chans), BF16),
@@ -351,7 +358,7 @@
             pltpu.VMEM((n, pixels + 8, chans), F32),
             pltpu.VMEM((2, pixels + 2 * HALO * cols, chans), BF16),
             pltpu.SemaphoreType.DMA((n,)),
-            pltpu.SemaphoreType.DMA((5,)),
+            pltpu.SemaphoreType.DMA((7,)),
             pltpu.SemaphoreType.DMA,
             pltpu.SemaphoreType.DMA,
             pltpu.SemaphoreType.DMA((n,)),

time: 21.3 us -> 21.3 us (level)
  no operation moved by 1% of the time
where the time goes in v2:
time: 21.3 us; the launch traced here: 21 us
  Pallas kernels  13.8 us (65%)
  local copies, waits for them, and re-layouts  7.14 us (34%)
    pallas_call x1, Pallas kernels, local(): pl.pallas_call(functools.partial(kernel, (n, slabs, rows, cols, dates, wi...  13.8 us
    unnamed x17, local copies, waits for them, and re-layouts  7.14 us

profile of v2, /device:TPU:0, one launch (start us, length us, event | category | flops | bytes accessed | tf_op | source)
XLA Modules:
  0.0 21.0 jit_solution(9964970257700558006)
XLA Ops:
  0.0 0.0 copy-start.6
  0.0 0.0 copy-start.7
  0.0 0.7 %copy-done.6 = s32[16]{0:T(128)S(1)} copy-done((s32[16]{0:T(128)S(1)}, s32[16]{0:T(128)}, u32[]{:S(2)}) %copy-start.6) | copy-done | bytes 88
  0.7 0.0 copy-done.7
  0.7 0.0 copy-start
  0.7 1.2 %copy-done = bf16[4,4,8,16,256]{4,3,2,1,0:T(8,128)(2,1)S(1)} copy-done((bf16[4,4,8,16,256]{4,3,2,1,0:T(8,128)(2,1)S(1)}, bf16[4,4,8,16,256]{4,3,2,1,0:T(8,128)(2,1)}, u32[]{:S(2)}) %copy-start) | copy-done | bytes 1048600
  1.9 0.0 copy-start.1
  1.9 1.1 %copy-done.1 = bf16[3,3,256,128]{3,2,1,0:T(8,128)(2,1)S(1)} copy-done((bf16[3,3,256,128]{3,2,1,0:T(8,128)(2,1)S(1)}, bf16[3,3,256,128]{3,2,1,0:T(8,128)(2,1)}, u32[]{:S(2)}) %copy-start.1) | copy-done | bytes 589848
  3.0 0.0 copy-start.2
  3.0 1.1 %copy-done.2 = bf16[3,3,256,128]{3,2,1,0:T(8,128)(2,1)S(1)} copy-done((bf16[3,3,256,128]{3,2,1,0:T(8,128)(2,1)S(1)}, bf16[3,3,256,128]{3,2,1,0:T(8,128)(2,1)}, u32[]{:S(2)}) %copy-start.2) | copy-done | bytes 589848
  4.0 0.0 copy-start.3
  4.0 0.8 %copy-done.3 = s32[4,4,8,16]{3,2,1,0:T(8,128)S(1)} copy-done((s32[4,4,8,16]{3,2,1,0:T(8,128)S(1)}, s32[4,4,8,16]{3,2,1,0:T(8,128)}, u32[]{:S(2)}) %copy-start.3) | copy-done | bytes 8216
  4.9 0.0 copy-start.4
  4.9 0.8 %copy-done.4 = bf16[256,128]{1,0:T(8,128)(2,1)S(1)} copy-done((bf16[256,128]{1,0:T(8,128)(2,1)S(1)}, bf16[256,128]{1,0:T(8,128)(2,1)}, u32[]{:S(2)}) %copy-start.4) | copy-done | bytes 65560
  5.7 0.0 copy-start.5
  5.7 0.8 %copy-done.5 = bf16[256,128]{1,0:T(8,128)(2,1)S(1)} copy-done((bf16[256,128]{1,0:T(8,128)(2,1)S(1)}, bf16[256,128]{1,0:T(8,128)(2,1)}, u32[]{:S(2)}) %copy-start.5) | copy-done | bytes 65560
  6.5 13.8 %shard_map.82 = bf16[32,128]{1,0:T(8,128)(2,1)S(1)} custom-call(bf16[4,512,256]{2,1,0:T(8,128)(2,1)S(1)} %bitcast.7, s32[4,32,16]{2,1,0:T(8,128)S(1)} %bitcast.10, s32[1,16]{1,0:T(1,128)S(1)} %bitcast.12, f32[1,128]{1,0:T(1,128)S(1)} %bitcast.13, bf16[256,128]{1,0:T(8,128)(2,1)S(1)} %copy-done.4, bf16[256,128]{1,0:T(8,128)(2,1)S(1)} %copy-done.5, ...), custom_call_target="tpu_custom_call" | custom-call | tf_op jit(solution)/shard_map/pallas_call | solution.py:341
  20.4 0.6 %copy.10 = bf16[1,4,8,128]{3,2,1,0:T(8,128)(2,1)} copy(bf16[1,4,8,128]{3,2,1,0:T(8,128)(2,1)S(1)} %bitcast.11) | data formatting | bytes 16384
Async XLA Ops:
  0.0 0.7 %copy-start.6 = (s32[16]{0:T(128)S(1)}, s32[16]{0:T(128)}, u32[]{:S(2)}) copy-start(s32[16]{0:T(128)} %param.10) | copy-start | bytes 196
  0.0 0.7 %copy-start.7 = (f32[128]{0:T(128)S(1)}, f32[128]{0:T(128)}, u32[]{:S(2)}) copy-start(f32[128]{0:T(128)} %param.11) | copy-start | bytes 1540
  0.7 1.2 %copy-start = (bf16[4,4,8,16,256]{4,3,2,1,0:T(8,128)(2,1)S(1)}, bf16[4,4,8,16,256]{4,3,2,1,0:T(8,128)(2,1)}, u32[]{:S(2)}) copy-start(bf16[4,4,8,16,256]{4,3,2,1,0:T(8,128)(2,1)} %param.8) | copy-start | bytes 3145732
  1.9 1.1 %copy-start.1 = (bf16[3,3,256,128]{3,2,1,0:T(8,128)(2,1)S(1)}, bf16[3,3,256,128]{3,2,1,0:T(8,128)(2,1)}, u32[]{:S(2)}) copy-start(bf16[3,3,256,128]{3,2,1,0:T(8,128)(2,1)} %param.14) | copy-start | bytes 1769476
  3.0 1.1 %copy-start.2 = (bf16[3,3,256,128]{3,2,1,0:T(8,128)(2,1)S(1)}, bf16[3,3,256,128]{3,2,1,0:T(8,128)(2,1)}, u32[]{:S(2)}) copy-start(bf16[3,3,256,128]{3,2,1,0:T(8,128)(2,1)} %param.15) | copy-start | bytes 1769476
  4.0 0.8 %copy-start.3 = (s32[4,4,8,16]{3,2,1,0:T(8,128)S(1)}, s32[4,4,8,16]{3,2,1,0:T(8,128)}, u32[]{:S(2)}) copy-start(s32[4,4,8,16]{3,2,1,0:T(8,128)} %param.9) | copy-start | bytes 24580
  4.9 0.8 %copy-start.4 = (bf16[256,128]{1,0:T(8,128)(2,1)S(1)}, bf16[256,128]{1,0:T(8,128)(2,1)}, u32[]{:S(2)}) copy-start(bf16[256,128]{1,0:T(8,128)(2,1)} %key_weight.1) | copy-start | bytes 196612
  5.7 0.8 %copy-start.5 = (bf16[256,128]{1,0:T(8,128)(2,1)S(1)}, bf16[256,128]{1,0:T(8,128)(2,1)}, u32[]{:S(2)}) copy-start(bf16[256,128]{1,0:T(8,128)(2,1)} %value_weight.1) | copy-start | bytes 196612

commit v3 on v2

--- a/solution.py
+++ b/solution.py
@@ -96,6 +96,8 @@
     enc_v,
     part_s,
     part_r,
+    low_r,
+    high_r,
     pool_v,
     tok_sem,
     in_sem,
@@ -119,6 +121,25 @@
     def tok_copy(tile):
         return pltpu.make_async_copy(tokens.at[tile], tok_v.at[tile], tok_sem.at[tile])
 
+    barrier = pltpu.get_barrier_semaphore()
+
+    def signal(where):
+        pl.semaphore_signal(barrier, inc=1, device_id=where, device_id_type=MESH)
+
+    @pl.loop(1, n)
+    def _(step):
+        signal({"date": lax.rem(date + step, n)})
+
+    for has, off in ((has_up, -1), (has_down, 1)):
+
+        @pl.when(has)
+        def _(off=off):
+            @pl.loop(0, n)
+            def _(step):
+                signal({"date": lax.rem(date + step, n), "tile": slab + off})
+
+    signal({"head": other})
+
     loads = [
         pltpu.make_async_copy(days, days_v, in_sem.at[0]),
         pltpu.make_async_copy(query, query_v, in_sem.at[1]),
@@ -137,22 +158,6 @@
 
     for load in loads[5:]:
         load.start()
-
-    barrier = pltpu.get_barrier_semaphore()
-
-    @pl.loop(1, n)
-    def _(step):
-        pl.semaphore_signal(barrier, inc=1, device_id={"date": lax.rem(date + step, n)}, device_id_type=MESH)
-
-    pl.semaphore_signal(barrier, inc=1, device_id={"head": other}, device_id_type=MESH)
-    for has, off in ((has_up, -1), (has_down, 1)):
-
-        @pl.when(has)
-        def _(off=off):
-            for core in range(2):
-                pl.semaphore_signal(
-                    barrier, inc=1, device_id={"tile": slab + off, "head": core}, device_id_type=MESH
-                )
 
     loads[0].wait()
     day_row = days_v[...].astype(F32)
@@ -174,31 +179,31 @@
     proj_v[:, 2 * chans :] = low
     loads[4].wait()
 
-    has_count = has_up.astype(jnp.int32) + has_down.astype(jnp.int32)
-    pl.semaphore_wait(barrier, n + 2 * has_count)
-
-    w1_copy = pltpu.make_async_remote_copy(
-        src_ref=conv_first,
-        dst_ref=w1_v.at[head],
-        send_sem=w1_send,
-        recv_sem=w1_recv,
-        device_id={"head": other},
-        device_id_type=MESH,
-    )
-    w1_copy.start()
-
     lane = iota((8, chans), 1) % HSIZE // 4
     ones = jnp.ones((dates, chans), BF16)
 
-    def part_copy(tile, slot):
+    halo = HALO * cols
+    ends = halo + 16
+
+    def part_copy(way, tile, slot):
+        start, count = ((0, pixels + 16), (0, ends), (pixels - halo, ends))[way]
         return pltpu.make_async_remote_copy(
-            src_ref=part_s.at[tile],
-            dst_ref=part_r.at[slot],
-            send_sem=part_send.at[tile],
-            recv_sem=part_recv.at[slot],
-            device_id={"date": tile},
+            src_ref=part_s.at[tile, pl.ds(start, count)],
+            dst_ref=(part_r, low_r, high_r)[way].at[slot],
+            send_sem=part_send.at[way, tile],
+            recv_sem=part_recv.at[way, slot],
+            device_id=({"date": tile}, {"date": tile, "tile": slab - 1}, {"date": tile, "tile": slab + 1})[way],
             device_id_type=MESH,
         )
+
+    def beside(fn):
+        @pl.when(has_up)
+        def _():
+            fn(1)
+
+        @pl.when(has_down)
+        def _():
+            fn(2)
 
     def attend(tile):
         feats = tok_v[tile].astype(F32).reshape(pixels, dates, width)
@@ -210,7 +215,7 @@
         score = both[:, chans : 2 * chans] + both[:, 2 * chans :] + cloud
         score = score.reshape(pixels, dates, chans)
         vals = both[:, :chans].reshape(pixels, dates, chans)
-        top = jnp.max(score, axis=1)
+        top = sum(term.astype(F32) for term in split(jnp.max(score, axis=1), 2))
         expo = jnp.exp(score - top[:, None, :])
         total = jnp.sum(expo, axis=1)
         sums = jnp.sum(expo * vals, axis=1)
@@ -219,102 +224,112 @@
         for group in range(groups):
             stats = jnp.where(lane == group, top[group * 8 : group * 8 + 8], stats)
             stats = jnp.where(lane == group + groups, total[group * 8 : group * 8 + 8], stats)
-        return sums, stats
+        part_s[tile, :halo] = sums[:halo].astype(BF16)
+        part_s[tile, halo:ends] = jnp.concatenate(split(stats, 2), axis=0)
+        part_s[tile, ends:] = sums[halo:].astype(BF16)
 
     @pl.loop(0, n - 1)
     def _(step):
         tile = tile_at(step)
         tok_copy(tile).wait()
-        sums, stats = attend(tile)
-        part_s[tile, :pixels] = sums
-        part_s[tile, pixels:] = stats
-        part_copy(tile, date).start()
+        attend(tile)
+
+    sides = has_up.astype(jnp.int32) + has_down.astype(jnp.int32)
+    pl.semaphore_wait(barrier, n + n * sides)
+
+    @pl.loop(0, n - 1)
+    def _(step):
+        part_copy(0, tile_at(step), date).start()
+        beside(lambda way: part_copy(way, tile_at(step), date).start())
 
     tok_copy(date).wait()
-    sums, stats = attend(date)
-    part_r[date, :pixels] = sums
-    part_r[date, pixels:] = stats
+    attend(date)
+    beside(lambda way: part_copy(way, date, date).start())
+    w1_copy = pltpu.make_async_remote_copy(
+        src_ref=conv_first,
+        dst_ref=w1_v.at[head],
+        send_sem=w1_send,
+        recv_sem=w1_recv,
+        device_id={"head": other},
+        device_id_type=MESH,
+    )
+    w1_copy.start()
+    part_r[date] = part_s[date]
+
+    groups = pixels // 8
+
+    def merge(parts, at, stat_at, first, count):
+        def stat_of(source):
+            both = parts[source, stat_at : stat_at + 16].astype(F32)
+            return both[:8] + both[8:]
+
+        stats = [stat_of(source) for source in range(n)]
+        best = functools.reduce(jnp.maximum, stats)
+        scales = [jnp.exp(stat - best) for stat in stats]
+        tots = sum(scale * pltpu.roll(stat, chans - HSIZE // 2, 1) for scale, stat in zip(scales, stats))
+        inverse = 1.0 / tots
+        total = jnp.zeros((8 * count, chans), F32)
+        for source in range(n):
+            weight = scales[source] * inverse
+            wides = []
+            for group in range(first, first + count):
+                wide = weight if group == 0 else pltpu.roll(weight, chans - 4 * group, 1)
+                wide = jnp.where(lane == 0, wide, 0.0)
+                for step in (4, 8, 16):
+                    wide = wide + pltpu.roll(wide, step, 1)
+                wides.append(wide)
+            sums = parts[source, at : at + 8 * count].astype(F32)
+            total = total + jnp.concatenate(wides, axis=0) * sums
+        return total.astype(BF16)
+
+    half = groups // 2
+
+    @pl.when(has_up)
+    def _():
+        @pl.loop(0, n)
+        def _(source):
+            part_copy(2, date, source).wait_recv()
+
+        pool_v[head, :halo] = merge(high_r, 16, 0, half, half)
+
+    @pl.when(has_down)
+    def _():
+        @pl.loop(0, n)
+        def _(source):
+            part_copy(1, date, source).wait_recv()
+
+        pool_v[head, halo + pixels :] = merge(low_r, 0, halo, 0, half)
 
     @pl.loop(1, n)
     def _(step):
-        part_copy(date, lax.rem(date + step, n)).wait_recv()
-
-    best = part_r[0, pixels:]
-    for source in range(1, n):
-        best = jnp.maximum(best, part_r[source, pixels:])
-    scales = []
-    tots = jnp.zeros((8, chans), F32)
-    for source in range(n):
-        stat = part_r[source, pixels:]
-        scale = jnp.exp(stat - best)
-        scales.append(scale)
-        tots = tots + scale * pltpu.roll(stat, chans - HSIZE // 2, 1)
-    inverse = 1.0 / tots
-    groups = pixels // 8
-    pooled = [jnp.zeros((8, chans), F32) for _ in range(groups)]
-    for source in range(n):
-        weight = scales[source] * inverse
-        for group in range(groups):
-            wide = weight if group == 0 else pltpu.roll(weight, chans - 4 * group, 1)
-            wide = jnp.where(lane == 0, wide, 0.0)
-            for step in (4, 8, 16):
-                wide = wide + pltpu.roll(wide, step, 1)
-            pooled[group] = pooled[group] + wide * part_r[source, group * 8 : group * 8 + 8]
-    halo = HALO * cols
-    pool_v[head, halo : halo + pixels] = jnp.concatenate(pooled, axis=0).astype(BF16)
-
-    def pool_copy(index, source, target, count, where):
-        return pltpu.make_async_remote_copy(
-            src_ref=pool_v.at[head, pl.ds(source, count)],
-            dst_ref=pool_v.at[head, pl.ds(target, count)],
-            send_sem=pool_send.at[index],
-            recv_sem=pool_recv.at[index],
-            device_id=where,
-            device_id_type=MESH,
-        )
-
-    def sends(fn):
-        fn(pool_copy(0, halo, halo, pixels, {"head": other}))
-
-        @pl.when(has_up)
-        def _():
-            for hop in range(2):
-                core = other if hop == 0 else head
-                fn(pool_copy(1 + hop, halo, halo + pixels, halo, {"tile": slab - 1, "head": core}))
-
-        @pl.when(has_down)
-        def _():
-            for hop in range(2):
-                core = other if hop == 0 else head
-                fn(pool_copy(3 + hop, pixels, 0, halo, {"tile": slab + 1, "head": core}))
-
-    sends(lambda copy: copy.start())
-
-    zeros = jnp.zeros((2, halo, chans), BF16)
+        part_copy(0, date, lax.rem(date + step, n)).wait_recv()
+
+    zeros = jnp.zeros((halo, chans), BF16)
 
     @pl.when(jnp.logical_not(has_up))
     def _():
-        pool_v[:, :halo] = zeros
+        pool_v[head, :halo] = zeros
 
     @pl.when(jnp.logical_not(has_down))
     def _():
-        pool_v[:, halo + pixels :] = zeros
-
+        pool_v[head, halo + pixels :] = zeros
+
+    pool_v[head, halo : 2 * halo] = merge(part_r, 0, halo, 0, half)
+    pool_v[head, 2 * halo : 3 * halo] = merge(part_r, ends, halo, half, half)
+
+    pool_copy = pltpu.make_async_remote_copy(
+        src_ref=pool_v.at[head],
+        dst_ref=pool_v.at[head],
+        send_sem=pool_send,
+        recv_sem=pool_recv,
+        device_id={"head": other},
+        device_id_type=MESH,
+    )
+    pool_copy.start()
     for load in loads[5:]:
         load.wait()
     w1_copy.wait()
-
-    pool_copy(0, halo, halo, pixels, {"head": other}).wait_recv()
-
-    @pl.when(has_down)
-    def _():
-        for hop in range(2):
-            pool_copy(1 + hop, halo, halo + pixels, halo, {"head": other}).wait_recv()
-
-    @pl.when(has_up)
-    def _():
-        for hop in range(2):
-            pool_copy(3 + hop, pixels, 0, halo, {"head": other}).wait_recv()
+    pool_copy.wait_recv()
 
     field = jnp.concatenate([pool_v[0], pool_v[1]], axis=1).astype(F32)
     first = jnp.concatenate([w1_v[0], w1_v[1]], axis=1)
@@ -326,9 +341,15 @@
 
     @pl.loop(0, n - 1)
     def _(step):
-        part_copy(tile_at(step), date).wait_send()
-
-    sends(lambda copy: copy.wait_send())
+        part_copy(0, tile_at(step), date).wait_send()
+
+    def sent(way):
+        @pl.loop(0, n)
+        def _(tile):
+            part_copy(way, tile, date).wait_send()
+
+    beside(sent)
+    pool_copy.wait_send()
 
 
 def local(n, slabs, tokens, cloud_mask, day_of_year, query, key_weight, value_weight, conv_first, conv_second):
@@ -354,20 +375,22 @@
             pltpu.VMEM((depth, chans), BF16),
             pltpu.VMEM((width, 3 * chans), BF16),
             pltpu.VMEM((dates, width), F32),
-            pltpu.VMEM((n, pixels + 8, chans), F32),
-            pltpu.VMEM((n, pixels + 8, chans), F32),
+            pltpu.VMEM((n, pixels + 16, chans), BF16),
+            pltpu.VMEM((n, pixels + 16, chans), BF16),
+            pltpu.VMEM((n, HALO * cols + 16, chans), BF16),
+            pltpu.VMEM((n, HALO * cols + 16, chans), BF16),
             pltpu.VMEM((2, pixels + 2 * HALO * cols, chans), BF16),
             pltpu.SemaphoreType.DMA((n,)),
             pltpu.SemaphoreType.DMA((7,)),
             pltpu.SemaphoreType.DMA,
             pltpu.SemaphoreType.DMA,
-            pltpu.SemaphoreType.DMA((n,)),
-            pltpu.SemaphoreType.DMA((n,)),
-            pltpu.SemaphoreType.DMA((5,)),
-            pltpu.SemaphoreType.DMA((5,)),
+            pltpu.SemaphoreType.DMA((3, n)),
+            pltpu.SemaphoreType.DMA((3, n)),
+            pltpu.SemaphoreType.DMA,
+            pltpu.SemaphoreType.DMA,
         ],
         compiler_params=pltpu.CompilerParams(
-            collective_id=0, has_side_effects=True, vmem_limit_bytes=48 * 1024 * 1024
+            collective_id=0, has_side_effects=True, vmem_limit_bytes=60 * 1024 * 1024
         ),
     )(
         tokens.reshape(tiles, pixels * dates, width),

time: 21.3 us -> 15 us (0.70)
  the two profiles are of different devices: /device:TPU:0 before, /device:TPU:1 now
where the time goes in v3:
time: 15 us; the launch traced here: 14.8 us
  Pallas kernels  13.5 us (90%)
  local copies, waits for them, and re-layouts  1.3 us (9%)
    pallas_call x1, Pallas kernels, local(): pl.pallas_call(functools.partial(kernel, (n, slabs, rows, cols, dates, wi...  13.5 us
    unnamed x1, local copies, waits for them, and re-layouts  1.3 us

profile of v3, /device:TPU:1, one launch (start us, length us, event | category | flops | bytes accessed | tf_op | source)
XLA Modules:
  0.0 14.8 jit_solution(3593793685078044690)
XLA Ops:
  0.0 13.5 %shard_map.82 = bf16[32,128]{1,0:T(8,128)(2,1)} custom-call(bf16[4,512,256]{2,1,0:T(8,128)(2,1)} %bitcast.7, s32[4,32,16]{2,1,0:T(8,128)} %bitcast.10, s32[1,16]{1,0:T(1,128)} %bitcast.12, f32[1,128]{1,0:T(1,128)} %bitcast.13, bf16[256,128]{1,0:T(8,128)(2,1)} %key_weight.1, bf16[256,128]{1,0:T(8,128)(2,1)} %value_weight.1, bf16[2304,128]{1,0:T(8,128)(2,1)} %bitcast.8, ...), custom_call_target="tpu_custom_call" | custom-call | tf_op jit(solution)/shard_map/pallas_call | solution.py:362
  13.5 1.3 %copy.10 = bf16[1,4,8,128]{3,2,1,0:T(8,128)(2,1)} copy(bf16[1,4,8,128]{3,2,1,0:T(8,128)(2,1)} %bitcast.11) | data formatting | bytes 16384

commit v4 on v3

--- a/solution.py
+++ b/solution.py
@@ -228,19 +228,21 @@
         part_s[tile, halo:ends] = jnp.concatenate(split(stats, 2), axis=0)
         part_s[tile, ends:] = sums[halo:].astype(BF16)
 
-    @pl.loop(0, n - 1)
-    def _(step):
-        tile = tile_at(step)
-        tok_copy(tile).wait()
-        attend(tile)
-
+    def send(step):
+        part_copy(0, tile_at(step), date).start()
+        beside(lambda way: part_copy(way, tile_at(step), date).start())
+
+    tok_copy(tile_at(0)).wait()
+    attend(tile_at(0))
     sides = has_up.astype(jnp.int32) + has_down.astype(jnp.int32)
     pl.semaphore_wait(barrier, n + n * sides)
-
-    @pl.loop(0, n - 1)
+    send(0)
+
+    @pl.loop(1, n - 1)
     def _(step):
-        part_copy(0, tile_at(step), date).start()
-        beside(lambda way: part_copy(way, tile_at(step), date).start())
+        tok_copy(tile_at(step)).wait()
+        attend(tile_at(step))
+        send(step)
 
     tok_copy(date).wait()
     attend(date)
@@ -284,6 +286,38 @@
 
     half = groups // 2
 
+    def pool_copy(index, start, count):
+        return pltpu.make_async_remote_copy(
+            src_ref=pool_v.at[head, pl.ds(start, count)],
+            dst_ref=pool_v.at[head, pl.ds(start, count)],
+            send_sem=pool_send.at[index],
+            recv_sem=pool_recv.at[index],
+            device_id={"head": other},
+            device_id_type=MESH,
+        )
+
+    high_copy = pool_copy(0, 0, halo)
+    own_copy = pool_copy(1, halo, pixels)
+    low_copy = pool_copy(2, halo + pixels, halo)
+
+    @pl.loop(1, n)
+    def _(step):
+        part_copy(0, date, lax.rem(date + step, n)).wait_recv()
+
+    pool_v[head, halo : 2 * halo] = merge(part_r, 0, halo, 0, half)
+    pool_v[head, 2 * halo : 3 * halo] = merge(part_r, ends, halo, half, half)
+    own_copy.start()
+
+    zeros = jnp.zeros((2, halo, chans), BF16)
+
+    @pl.when(jnp.logical_not(has_up))
+    def _():
+        pool_v[:, :halo] = zeros
+
+    @pl.when(jnp.logical_not(has_down))
+    def _():
+        pool_v[:, halo + pixels :] = zeros
+
     @pl.when(has_up)
     def _():
         @pl.loop(0, n)
@@ -291,6 +325,7 @@
             part_copy(2, date, source).wait_recv()
 
         pool_v[head, :halo] = merge(high_r, 16, 0, half, half)
+        high_copy.start()
 
     @pl.when(has_down)
     def _():
@@ -299,37 +334,20 @@
             part_copy(1, date, source).wait_recv()
 
         pool_v[head, halo + pixels :] = merge(low_r, 0, halo, 0, half)
-
-    @pl.loop(1, n)
-    def _(step):
-        part_copy(0, date, lax.rem(date + step, n)).wait_recv()
-
-    zeros = jnp.zeros((halo, chans), BF16)
-
-    @pl.when(jnp.logical_not(has_up))
-    def _():
-        pool_v[head, :halo] = zeros
-
-    @pl.when(jnp.logical_not(has_down))
-    def _():
-        pool_v[head, halo + pixels :] = zeros
-
-    pool_v[head, halo : 2 * halo] = merge(part_r, 0, halo, 0, half)
-    pool_v[head, 2 * halo : 3 * halo] = merge(part_r, ends, halo, half, half)
-
-    pool_copy = pltpu.make_async_remote_copy(
-        src_ref=pool_v.at[head],
-        dst_ref=pool_v.at[head],
-        send_sem=pool_send,
-        recv_sem=pool_recv,
-        device_id={"head": other},
-        device_id_type=MESH,
-    )
-    pool_copy.start()
+        low_copy.start()
+
     for load in loads[5:]:
         load.wait()
     w1_copy.wait()
-    pool_copy.wait_recv()
+    own_copy.wait_recv()
+
+    @pl.when(has_up)
+    def _():
+        high_copy.wait_recv()
+
+    @pl.when(has_down)
+    def _():
+        low_copy.wait_recv()
 
     field = jnp.concatenate([pool_v[0], pool_v[1]], axis=1).astype(F32)
     first = jnp.concatenate([w1_v[0], w1_v[1]], axis=1)
@@ -349,7 +367,15 @@
             part_copy(way, tile, date).wait_send()
 
     beside(sent)
-    pool_copy.wait_send()
+    own_copy.wait_send()
+
+    @pl.when(has_up)
+    def _():
+        high_copy.wait_send()
+
+    @pl.when(has_down)
+    def _():
+        low_copy.wait_send()
 
 
 def local(n, slabs, tokens, cloud_mask, day_of_year, query, key_weight, value_weight, conv_first, conv_second):
@@ -386,8 +412,8 @@
             pltpu.SemaphoreType.DMA,
             pltpu.SemaphoreType.DMA((3, n)),
             pltpu.SemaphoreType.DMA((3, n)),
-            pltpu.SemaphoreType.DMA,
-            pltpu.SemaphoreType.DMA,
+            pltpu.SemaphoreType.DMA((3,)),
+            pltpu.SemaphoreType.DMA((3,)),
         ],
         compiler_params=pltpu.CompilerParams(
             collective_id=0, has_side_effects=True, vmem_limit_bytes=60 * 1024 * 1024

time: 15 us -> 14 us (0.933)
  Pallas kernels: 13.5 us -> 12.5 us
    pallas_call x1, Pallas kernels: 13.5 us -> 12.5 us  [local(): pl.pallas_call(functools.partial(kernel, (n, slabs, rows, cols, dates, wi...]
where the time goes in v4:
time: 14 us; the launch traced here: 13.8 us
  Pallas kernels  12.5 us (89%)
  local copies, waits for them, and re-layouts  1.3 us (9%)
    pallas_call x1, Pallas kernels, local(): pl.pallas_call(functools.partial(kernel, (n, slabs, rows, cols, dates, wi...  12.5 us
    unnamed x1, local copies, waits for them, and re-layouts  1.3 us

profile of v4, /device:TPU:1, one launch (start us, length us, event | category | flops | bytes accessed | tf_op | source)
XLA Modules:
  0.0 13.8 jit_solution(17467029004031937481)
XLA Ops:
  0.0 12.5 %shard_map.82 = bf16[32,128]{1,0:T(8,128)(2,1)} custom-call(bf16[4,512,256]{2,1,0:T(8,128)(2,1)} %bitcast.7, s32[4,32,16]{2,1,0:T(8,128)} %bitcast.10, s32[1,16]{1,0:T(1,128)} %bitcast.12, f32[1,128]{1,0:T(1,128)} %bitcast.13, bf16[256,128]{1,0:T(8,128)(2,1)} %key_weight.1, bf16[256,128]{1,0:T(8,128)(2,1)} %value_weight.1, bf16[2304,128]{1,0:T(8,128)(2,1)} %bitcast.8, ...), custom_call_target="tpu_custom_call" | custom-call | tf_op jit(solution)/shard_map/pallas_call | solution.py:388
  12.5 1.3 %copy.10 = bf16[1,4,8,128]{3,2,1,0:T(8,128)(2,1)} copy(bf16[1,4,8,128]{3,2,1,0:T(8,128)(2,1)} %bitcast.11) | data formatting | bytes 16384
